TPU v7x, 128 devices: a whole 4x4x4 slice. The times are simulated.
128 devices in a mesh: grp: 4 (over x), gx: 4 (over z_lo, core), gy: 8 (over z_hi, y).
Axes of the slice: x: 4, y: 4, z: 4 (z_hi: 2, z_lo: 2; z = z_hi * 2 + z_lo), core: 2. Of those that a mesh axis runs over, the one named last changes fastest.
Arguments:
- flow_state: float32 [8, 768, 128, 128], P(None, ('grp', 'gx'), 'gy'), may hold values from -90 to 90
- speeds: float32 [3, 8], replicated, may hold values from 0.3 to 1.2
- viscosity: float32 [8], replicated, may hold values from 0.02 to 0.2
- reaction: float32 [8, 8], replicated, may hold values from -2 to 2
- start_basis: float32 [768, 96], replicated, may hold values from -6 to 6
- slab_table: int32 [8, 8, 1], replicated, may hold values from 0 to 15; in each aligned block of 8 rows (0 to 7, 8 to 15, ..., all dimensions but the last counted through in order) at most 2 rows name the same one
Outputs:
- final_state: float32 [8, 768, 128, 128], P(None, ('grp', 'gx'), 'gy')
- core_slots: float32 [256, 96, 8, 2, 128], P(('grp', 'gx', 'gy'))
Inputs may be any that keep to these rules, and one draw needn't show every extreme that they name: slab_table[t, u, 0] names the slab that stores unit u of row t; within each row t no slab is named by more than 2 units, a bound that some block reaches.
All inputs are finite; a program needn't handle non-finite values.
Results may differ from a plain program's by a relative error of at most 0.0034.
Values may be sent and summed in bfloat16 or wider, within the bound.
A program may use at most 256 MiB of HBM per device.

v0:
```python
import jax
import jax.numpy as jnp
from jax import lax
from jax.sharding import PartitionSpec as P

V = 8
NX = 768
R = 96
NZ = 128
YB = 2
NEWTON = 5
slope_weights = (0.8, -0.2, 4.0 / 105.0, -1.0 / 280.0)
curve_weights = (1.6, -0.2, 8.0 / 315.0, -1.0 / 560.0)
curve_center = -205.0 / 72.0
time_step = 0.2


def extended(shard, sides, width):
    for axis, dim in sides:
        peers, length = (lax.axis_size(axis), shard.shape[dim])
        up = [(i, (i + 1) % peers) for i in range(peers)]
        down = [(j, i) for i, j in up]
        last = lax.slice_in_dim(shard, length - width, length, axis=dim)
        initial = lax.slice_in_dim(shard, 0, width, axis=dim)
        before = lax.ppermute(last, axis, up)
        after = lax.ppermute(initial, axis, down)
        shard = jnp.concatenate([before, shard, after], axis=dim)
    return shard


def tendency(padded, speeds, viscosity, reaction):
    center = padded[:, 4:-4, 4:-4, :]
    width_first = center.shape[1]
    width_second = center.shape[2]
    diffusion = viscosity[:, None, None, None]
    speed_one = speeds[0][:, None, None, None]
    speed_two = speeds[1][:, None, None, None]
    speed_three = speeds[2][:, None, None, None]
    summed = 3.0 * curve_center * diffusion * center
    summed = summed + jnp.einsum("kj,jxyz->kxyz", reaction, center, precision=lax.Precision.HIGHEST)
    for offset in range(1, 5):
        slope_weight = slope_weights[offset - 1]
        curve_weight = curve_weights[offset - 1]
        spread = curve_weight * diffusion
        summed = summed + (
            (spread - slope_weight * speed_one)
            * padded[:, 4 + offset : 4 + offset + width_first, 4 : 4 + width_second, :]
            + (spread + slope_weight * speed_one)
            * padded[:, 4 - offset : 4 - offset + width_first, 4 : 4 + width_second, :]
            + (spread - slope_weight * speed_two)
            * padded[:, 4 : 4 + width_first, 4 + offset : 4 + offset + width_second, :]
            + (spread + slope_weight * speed_two)
            * padded[:, 4 : 4 + width_first, 4 - offset : 4 - offset + width_second, :]
            + (spread - slope_weight * speed_three) * jnp.roll(center, -offset, 3)
            + (spread + slope_weight * speed_three) * jnp.roll(center, offset, 3)
        )
    return summed


def extend(field):
    return extended(field, ((("grp", "gx"), 1), ("gy", 2)), 4)


def on_device(flow_state, speeds, viscosity, reaction, start_basis, slab_table):
    first = flow_state + time_step * tendency(extend(flow_state), speeds, viscosity, reaction)
    final_state = 0.5 * flow_state + 0.5 * (
        first + time_step * tendency(extend(first), speeds, viscosity, reaction)
    )
    snapshot = final_state.astype(jnp.bfloat16)
    tile_rows = flow_state.shape[1]
    unit_count = flow_state.shape[2] // YB
    slab_count = lax.axis_size(("grp", "gx"))
    capacity = max(2, 3 * unit_count // slab_count)
    columns = V * YB * NZ
    table_row = lax.dynamic_index_in_dim(
        slab_table[:, :, 0], lax.axis_index("gy"), 0, keepdims=False
    )
    order = jnp.arange(unit_count, dtype=jnp.int32)
    earlier = order[None, :] < order[:, None]
    same_slab = table_row[:, None] == table_row[None, :]
    slot_index = jnp.sum((same_slab & earlier).astype(jnp.int32), axis=1)
    target = table_row * capacity + slot_index
    placing = (
        jnp.arange(slab_count * capacity, dtype=jnp.int32)[:, None] == target[None, :]
    ).astype(jnp.bfloat16)
    blocks = snapshot.reshape(V, tile_rows, unit_count, YB, NZ)
    outgoing = jnp.einsum(
        "pu,vxuyz->pxvyz", placing, blocks, preferred_element_type=jnp.float32
    ).astype(jnp.bfloat16)
    received = lax.all_to_all(
        outgoing.reshape(slab_count, capacity, tile_rows, columns),
        ("grp", "gx"),
        split_axis=0,
        concat_axis=2,
        tiled=True,
    )
    received = received.reshape(capacity, NX, columns)
    partial_value = lax.dot_general(
        received, received, (((0, 2), (0, 2)), ((), ())), preferred_element_type=jnp.float32
    )
    gram = lax.psum(partial_value, ("grp", "gx", "gy"))
    product = jnp.dot(gram, start_basis, precision=lax.Precision.HIGHEST)
    basis = product / jnp.sqrt(jnp.sum(product * product))
    for repeat in range(NEWTON):
        inner_gram = jnp.dot(basis.T, basis, precision=lax.Precision.HIGHEST)
        basis = 1.5 * basis - 0.5 * jnp.dot(basis, inner_gram, precision=lax.Precision.HIGHEST)
    basis_half = basis.astype(jnp.bfloat16)
    cores = jnp.einsum("xr,mxc->mrc", basis_half, received, preferred_element_type=jnp.float32)
    return (final_state, cores.reshape(capacity, R, V, YB, NZ))


def solution(mesh):
    placed = (P(None, ("grp", "gx"), "gy", None), P(), P(), P(), P(), P())
    return jax.shard_map(
        on_device,
        mesh=mesh,
        in_specs=placed,
        out_specs=(
            P(None, ("grp", "gx"), "gy", None),
            P(("grp", "gx", "gy"), None, None, None, None),
        ),
        check_vma=False,
    )
```

profile of v0, /device:TPU:1, one launch (start us, length us, event | category | flops | bytes accessed | tf_op | source)
XLA Modules:
  0.0 518.8 jit_solution(14506563445527793642)
XLA Ops:
  7.2 1.1 fusion.116
  8.3 0.9 copy.103
  9.2 3.0 collective-permute-start.1
  12.2 0.9 copy.104
  13.1 5.8 %fusion.114 = (f32[8,48,16,1]{3,2,1,0:T(8,128)S(1)}, f32[8,48,16,1]{3,2,1,0:T(8,128)}) fusion(f32[8,48,16,128]{3,2,1,0:T(8,128)} %param.6), kind=kLoop, calls=%fused_computation.230 | loop fusion | bytes 98304 | tf_op jit(solution)/shard_map/jit(_roll_static)/slice | solution.py:55
  18.9 3.9 fusion.115
  22.7 1.1 fusion.112
  23.8 3.7 fusion.113
  27.5 1.1 fusion.110
  28.6 1.1 fusion.111
  29.7 1.1 fusion.108
  30.8 1.8 constant_dynamic-update-slice_fusion.3
  32.6 5.7 %constant_dynamic-update-slice_fusion.1 = (f32[8,52,16,128]{3,0,2,1:T(8,128)}, f32[8,52,16,128]{3,0,2,1:T(8,128)}, f32[8,56,16,128]{3,0,2,1:T(8,128)}) fusion(f32[8,48,16,128]{3,2,1,0:T(8,128)S(1)} %copy-done.1, f32[8,52,16,128]{3,0,2,1:T(8,128)} %get-tuple-element.55, f32[8,56,16,128]{3,0,2,1:T(8,128)} %get-tuple-element.56), kind=kLoop, calls=%fused_computation.168 | loop fusion | bytes 12582912
  38.3 0.8 constant_dynamic-update-slice_fusion
  39.2 2.9 fusion.98
  42.0 5.8 %collective-permute-start.2 = (f32[8,56,4,128]{3,0,2,1:T(8,128)}, f32[8,56,4,128]{3,0,2,1:T(8,128)}, u32[]{:S(2)}, u32[]{:S(2)}) collective-permute-start(f32[8,56,4,128]{3,0,2,1:T(8,128)} %get-tuple-element.12), channel_id=1, source_target_pairs={{1,0},{2,1},{3,2},{4,3},{5,4},{6,5},{7,6},{0,7},{9,8},{10,9},{11,1... | collective-permute-start | bytes 2752520 | tf_op jit(solution)/shard_map/ppermute | solution.py:26
  47.9 3.8 fusion.109
  51.7 5.6 %copy.105 = f32[8,48,16,1]{3,0,2,1:T(8,128)} copy(f32[8,48,16,1]{3,2,1,0:T(8,128)} %get-tuple-element.45) | data formatting | bytes 49152
  57.3 3.5 copy.106
  60.8 3.5 copy.107
  64.3 3.5 copy.108
  67.8 3.5 copy.109
  71.4 3.7 copy.110
  75.1 3.4 copy.111
  78.5 3.5 copy.112
  82.0 3.5 copy.113
  85.4 3.4 copy.114
  88.9 3.5 copy.115
  92.4 3.8 copy.116
  96.2 3.5 copy.117
  99.8 3.4 copy.118
  103.2 3.5 copy.119
  106.7 3.4 copy.120
  110.1 0.7 dynamic-slice_bitcast_fusion
  111.0 0.7 multiply_add_fusion
  111.7 37.7 %fusion.43 = f32[8,48,16,128]{3,0,2,1:T(8,128)S(1)} fusion(f32[8,56,16,128]{3,0,2,1:T(8,128)} %get-tuple-element.54, f32[8,56,4,128]{3,0,2,1:T(8,128)} %collective-permute-done.3, f32[8,56,4,128]{3,0,2,1:T(8,128)} %collective-permute-done.2, f32[8,52,16,128]{3,0,2,1:T(8,128)} %get-tuple-element.49, f32[8,52,16,128]{3,0,2,1:T(8,128)} %get-tuple-element.53, ...), kind=kOutput, calls=%fused_computation.70 | convolution fusion | flops 128974848 | bytes 90440736 | tf_op jit(solution)/shard_map/kj,jxyz->kxyz/dot_general | solution.py:40
  149.5 3.8 fusion.99
  153.3 3.8 fusion.100
  157.1 3.8 fusion.101
  161.0 3.9 fusion.102
  164.9 3.8 fusion.103
  168.6 2.8 collective-permute-start.4
  171.4 3.9 fusion.104
  175.3 2.1 collective-permute-done.5
  177.6 5.4 %collective-permute-start.6 = (f32[8,56,4,128]{3,0,2,1:T(8,128)S(1)}, f32[8,56,4,128]{3,0,2,1:T(8,128)S(1)}, u32[]{:S(2)}, u32[]{:S(2)}) collective-permute-start(f32[8,56,4,128]{3,0,2,1:T(8,128)S(1)} %get-tuple-element.10), channel_id=1, source_target_pairs={{1,0},{2,1},{3,2},{4,3},{5,4},{6,5},{7,6},{0,7},{9,8},{10,9},{11,1... | collective-permute-start | bytes 2752520 | tf_op jit(solution)/shard_map/ppermute | solution.py:26
  183.2 3.7 fusion.105
  187.0 3.9 fusion.106
  190.8 9.9 %collective-permute-done.6 = f32[8,56,4,128]{3,0,2,1:T(8,128)S(1)} collective-permute-done((f32[8,56,4,128]{3,0,2,1:T(8,128)S(1)}, f32[8,56,4,128]{3,0,2,1:T(8,128)S(1)}, u32[]{:S(2)}, u32[]{:S(2)}) %collective-permute-start.6) | collective-permute-done | bytes 917536 | tf_op jit(solution)/shard_map/ppermute | solution.py:26
  200.8 5.7 %collective-permute-done.7 = f32[8,56,4,128]{3,0,2,1:T(8,128)S(1)} collective-permute-done((f32[8,56,4,128]{3,0,2,1:T(8,128)S(1)}, f32[8,56,4,128]{3,0,2,1:T(8,128)S(1)}, u32[]{:S(2)}, u32[]{:S(2)}) %collective-permute-start.7) | collective-permute-done | bytes 917536 | tf_op jit(solution)/shard_map/ppermute | solution.py:25
  206.5 3.9 pad_maximum_fusion
  210.4 25.6 %fusion.117 = (bf16[8,48,16,128]{3,0,2,1:T(8,128)(2,1)S(1)}, f32[8,48,16,128]{3,0,2,1:T(8,128)}) fusion(f32[8,48,16,128]{3,0,2,1:T(8,128)S(1)} %fusion.43, f32[8,48,16,124]{3,0,2,1:T(8,128)} %get-tuple-element.16, f32[8,48,16,4]{3,0,2,1:T(8,128)} %get-tuple-element.14, f32[8]{0:T(128)S(1)} %get-tuple-element.62, f32[8,48,16,4]{3,0,2,1:T(8,128)} %get-tuple-element.15, ...), kind=kOutput, calls=%fused_computation.233 | convolution fusion | flops 131334144 | bytes 65028608 | tf_op jit(solution)/shard_map/kj,jxyz->kxyz/dot_general | solution.py:40
  236.0 1.9 convert_bitcast_fusion
  237.9 10.6 %copy.90 = bf16[32,48,8,2,128]{4,3,2,1,0:T(2,128)(2,1)} copy(bf16[32,48,8,2,128]{4,0,3,1,2:T(8,128)(2,1)S(1)} %convert_bitcast_fusion) | data formatting | bytes 12582912 | tf_op jit(solution)/shard_map/convert_element_type | solution.py:89
  248.6 11.1 %reshape.133 = bf16[16,2,48,2048]{3,2,1,0:T(8,128)(2,1)} reshape(bf16[32,48,8,2,128]{4,3,2,1,0:T(2,128)(2,1)} %copy.90) | data formatting | bytes 12582912 | tf_op jit(solution)/shard_map/reshape | solution.py:91
  259.7 78.8 %all_to_all.15 = bf16[16,2,48,2048]{3,2,1,0:T(8,128)(2,1)S(1)} all-to-all(bf16[16,2,48,2048]{3,2,1,0:T(8,128)(2,1)} %reshape.133), channel_id=1, replica_groups=mesh['grp'=4,'gx'=4,'gy'=8] {'grp','gx'}, dimensions={0} | all-to-all | bytes 12582912 | tf_op jit(solution)/shard_map/all_to_all | solution.py:90
  338.5 1.1 copy.91
  339.6 2.7 copy-done.3
  342.3 6.5 %convolution_bitcast_fusion.1 = f32[768,768]{1,0:T(8,128)} fusion(bf16[2,768,2048]{2,1,0:T(8,128)(2,1)S(1)} %bitcast.95), kind=kOutput, calls=%fused_computation.147 | convolution fusion | flops 4831838208 | bytes 8650752 | tf_op jit(solution)/shard_map/dot_general | solution.py:98
  348.8 2.2 copy.92
  351.0 144.7 %all-reduce.2.cloned.1.call-done = f32[768,768]{1,0:T(8,128)} async-done(((f32[768,768]{1,0:T(8,128)}), f32[768,768]{1,0:T(8,128)}) %all-reduce.2.cloned.1.call-update) | async-done | bytes 2359312 | tf_op jit(solution)/shard_map/psum | solution.py:101
  495.8 4.6 multiply_reduce_fusion
  502.3 0.5 fusion.86
  505.4 4.0 convolution_bitcast_fusion
  509.4 2.5 reshape.135
  (56 shorter events, 4.7 us)
Async XLA Ops:
  7.2 488.6 %copy-start = (f32[768,96]{0,1:T(8,128)S(1)}, f32[768,96]{0,1:T(8,128)}, u32[]{:S(2)}) copy-start(f32[768,96]{0,1:T(8,128)} %param.10) | copy-start | bytes 884740
  7.2 488.6 %all-reduce.2.cloned.1.call-start = ((), (), s32[]{:S(2)}) async-start(), calls=%async_computation.1 | async-start | bytes 4718592 | tf_op jit(solution)/shard_map/psum | solution.py:101
  9.2 21.6 %collective-permute-start.1 = (f32[8,4,16,128]{3,0,2,1:T(8,128)}, f32[8,4,16,128]{3,0,2,1:T(8,128)}, u32[]{:S(2)}, u32[]{:S(2)}) collective-permute-start(f32[8,4,16,128]{3,0,2,1:T(8,128)} %copy.103), channel_id=1, source_target_pairs={{0,8},{8,16},{16,24},{24,32},{32,40},{40,48},{48,56},{56,64},{64,7... | collective-permute-start | bytes 786440 | tf_op jit(solution)/shard_map/ppermute | solution.py:25
  13.1 5.8 %copy-start.1 = (f32[8,48,16,128]{3,2,1,0:T(8,128)S(1)}, f32[8,48,16,128]{3,2,1,0:T(8,128)}, u32[]{:S(2)}) copy-start(f32[8,48,16,128]{3,2,1,0:T(8,128)} %param.6) | copy-start | bytes 9437188
  13.1 25.2 %collective-permute-start = (f32[8,4,16,128]{3,0,2,1:T(8,128)}, f32[8,4,16,128]{3,0,2,1:T(8,128)S(1)}, u32[]{:S(2)}, u32[]{:S(2)}) collective-permute-start(f32[8,4,16,128]{3,0,2,1:T(8,128)} %copy.104), channel_id=1, source_target_pairs={{8,0},{16,8},{24,16},{32,24},{40,32},{48,40},{56,48},{64,56},{72,6... | collective-permute-start | bytes 786440 | tf_op jit(solution)/shard_map/ppermute | solution.py:26
  42.0 69.7 %collective-permute-start.2 = (f32[8,56,4,128]{3,0,2,1:T(8,128)}, f32[8,56,4,128]{3,0,2,1:T(8,128)}, u32[]{:S(2)}, u32[]{:S(2)}) collective-permute-start(f32[8,56,4,128]{3,0,2,1:T(8,128)} %get-tuple-element.12), channel_id=1, source_target_pairs={{1,0},{2,1},{3,2},{4,3},{5,4},{6,5},{7,6},{0,7},{9,8},{10,9},{11,1... | collective-permute-start | bytes 2752520 | tf_op jit(solution)/shard_map/ppermute | solution.py:26
  47.8 63.9 %collective-permute-start.3 = (f32[8,56,4,128]{3,0,2,1:T(8,128)}, f32[8,56,4,128]{3,0,2,1:T(8,128)}, u32[]{:S(2)}, u32[]{:S(2)}) collective-permute-start(f32[8,56,4,128]{3,0,2,1:T(8,128)} %get-tuple-element.13), channel_id=1, source_target_pairs={{0,1},{1,2},{2,3},{3,4},{4,5},{5,6},{6,7},{7,0},{8,9},{9,10},{10,1... | collective-permute-start | bytes 2752520 | tf_op jit(solution)/shard_map/ppermute | solution.py:25
  51.7 5.6 %copy-start.7 = (f32[8,48,16,127]{3,2,1,0:T(8,128)S(1)}, f32[8,48,16,127]{3,2,1,0:T(8,128)}, u32[]{:S(2)}) copy-start(f32[8,48,16,127]{3,2,1,0:T(8,128)} %get-tuple-element.47) | copy-start | bytes 9363460
  57.3 3.5 copy-start.6
  67.8 3.6 copy-start.5
  71.4 3.7 copy-start.4
  96.2 3.5 copy-start.9
  99.7 3.4 copy-start.8
  106.7 4.9 copy-start.13
  106.7 4.9 copy-start.14
  106.7 5.0 copy-start.15
  168.6 6.6 %collective-permute-start.4 = (f32[8,4,16,128]{3,0,2,1:T(8,128)S(1)}, f32[8,4,16,128]{3,0,2,1:T(8,128)S(1)}, u32[]{:S(2)}, u32[]{:S(2)}) collective-permute-start(f32[8,4,16,128]{3,0,2,1:T(8,128)S(1)} %get-tuple-element.30), channel_id=1, source_target_pairs={{8,0},{16,8},{24,16},{32,24},{40,32},{48,40},{56,48},{64,56},{72,6... | collective-permute-start | bytes 786440 | tf_op jit(solution)/shard_map/ppermute | solution.py:26
  171.4 6.0 %collective-permute-start.5 = (f32[8,4,16,128]{3,0,2,1:T(8,128)S(1)}, f32[8,4,16,128]{3,0,2,1:T(8,128)S(1)}, u32[]{:S(2)}, u32[]{:S(2)}) collective-permute-start(f32[8,4,16,128]{3,0,2,1:T(8,128)S(1)} %get-tuple-element.31), channel_id=1, source_target_pairs={{0,8},{8,16},{16,24},{24,32},{32,40},{40,48},{48,56},{56,64},{64,7... | collective-permute-start | bytes 786440 | tf_op jit(solution)/shard_map/ppermute | solution.py:25
  175.3 31.2 %copy-start.11 = (f32[8,4,16,128]{3,0,2,1:T(8,128)}, f32[8,4,16,128]{3,0,2,1:T(8,128)S(1)}, u32[]{:S(2)}) copy-start(f32[8,4,16,128]{3,0,2,1:T(8,128)S(1)} %collective-permute-done.4) | copy-start | bytes 786436
  177.4 29.1 %copy-start.12 = (f32[8,4,16,128]{3,0,2,1:T(8,128)}, f32[8,4,16,128]{3,0,2,1:T(8,128)S(1)}, u32[]{:S(2)}) copy-start(f32[8,4,16,128]{3,0,2,1:T(8,128)S(1)} %collective-permute-done.5) | copy-start | bytes 786436
  177.6 23.2 %collective-permute-start.6 = (f32[8,56,4,128]{3,0,2,1:T(8,128)S(1)}, f32[8,56,4,128]{3,0,2,1:T(8,128)S(1)}, u32[]{:S(2)}, u32[]{:S(2)}) collective-permute-start(f32[8,56,4,128]{3,0,2,1:T(8,128)S(1)} %get-tuple-element.10), channel_id=1, source_target_pairs={{1,0},{2,1},{3,2},{4,3},{5,4},{6,5},{7,6},{0,7},{9,8},{10,9},{11,1... | collective-permute-start | bytes 2752520 | tf_op jit(solution)/shard_map/ppermute | solution.py:26
  183.0 23.5 %collective-permute-start.7 = (f32[8,56,4,128]{3,0,2,1:T(8,128)S(1)}, f32[8,56,4,128]{3,0,2,1:T(8,128)S(1)}, u32[]{:S(2)}, u32[]{:S(2)}) collective-permute-start(f32[8,56,4,128]{3,0,2,1:T(8,128)S(1)} %get-tuple-element.11), channel_id=1, source_target_pairs={{0,1},{1,2},{2,3},{3,4},{4,5},{5,6},{6,7},{7,0},{8,9},{9,10},{10,1... | collective-permute-start | bytes 2752520 | tf_op jit(solution)/shard_map/ppermute | solution.py:25
  190.8 19.6 %copy-start.2 = (f32[8,48,16,128]{3,2,1,0:T(8,128)S(1)}, f32[8,48,16,128]{3,2,1,0:T(8,128)}, u32[]{:S(2)}) copy-start(f32[8,48,16,128]{3,2,1,0:T(8,128)} %param.6) | copy-start | bytes 9437188
  339.6 2.7 copy-start.3
  342.3 6.5 %copy-start.10 = (f32[8,48,16,128]{3,0,2,1:T(8,128)S(1)}, f32[8,48,16,128]{3,0,2,1:T(8,128)}, u32[]{:S(2)}) copy-start(f32[8,48,16,128]{3,0,2,1:T(8,128)} %get-tuple-element.83) | copy-start | bytes 9437188
Sparse Core Ops, SparseCore 0:
  348.9 146.8 all-reduce.1
where the time goes:
time: 528 us; the launch traced here: 519 us
  waiting for transfers between devices  163 us (31%)
  local copies, waits for them, and re-layouts  155 us (29%)
  matrix products  84.6 us (16%)
  blocking collectives  78.8 us (15%)
  starting transfers between devices  17.4 us (3%)
  between operations  15.1 us (3%)
    psum x1, waiting for transfers between devices, on_device(): gram = lax.psum(partial_value, ('grp', 'gx', 'gy'))  145 us
    all_to_all x1, blocking collectives, on_device(): lax.all_to_all(outgoing.reshape(slab_count, capacity, tile_rows, columns)...  78.8 us
    unnamed x53, local copies, waits for them, and re-layouts  72.6 us
    dot_general x2, matrix products, tendency(): jnp.einsum('kj,jxyz->kxyz', reaction, center, precision=lax.Precision.HIG...  63.4 us
    slice x16, local copies, waits for them, and re-layouts, tendency(): jnp.roll(center, offset, 3)  52 us
    ppermute x4, starting transfers between devices, extended(): after = lax.ppermute(initial, axis, down)  13.9 us
    reshape x1, local copies, waits for them, and re-layouts, on_device(): outgoing.reshape(slab_count, capacity, tile_rows, columns)  11.1 us
    convert_element_type x1, local copies, waits for them, and re-layouts, on_device(): outgoing = jnp.einsum('pu,vxuyz->pxvyz', placing, blocks, preferred_eleme...  10.6 us
  transfers between devices with their start and end apart: 9, of which 4 were waited for; matrix products, arithmetic and copies ran while one was open for 20% of the time, Pallas kernels for 0%

commit v1 on v0

--- a/solution.py
+++ b/solution.py
@@ -87,12 +87,20 @@
     outgoing = jnp.einsum(
         "pu,vxuyz->pxvyz", placing, blocks, preferred_element_type=jnp.float32
     ).astype(jnp.bfloat16)
-    received = lax.all_to_all(
-        outgoing.reshape(slab_count, capacity, tile_rows, columns),
-        ("grp", "gx"),
-        split_axis=0,
-        concat_axis=2,
-        tiled=True,
+    received = jnp.concatenate(
+        lax.all_to_all(
+            jnp.stack(
+                jnp.split(
+                    outgoing.reshape(slab_count, capacity, tile_rows, columns),
+                    lax.axis_size(("grp", "gx")),
+                    axis=0,
+                )
+            ),
+            ("grp", "gx"),
+            0,
+            0,
+        ),
+        axis=2,
     )
     received = received.reshape(capacity, NX, columns)
     partial_value = lax.dot_general(

time: 528 us -> 572 us (1.083)
  local copies, waits for them, and re-layouts: 155 us -> 200 us
    another operation x0 -> x17, local copies, waits for them, and re-layouts: none -> 27.4 us  [on_device(): jnp.stack(jnp.split(outgoing.reshape(slab_count, capacity, tile_rows, col...]
    split x0 -> x17, local copies, waits for them, and re-layouts: none -> 25.5 us  [on_device(): jnp.split(outgoing.reshape(slab_count, capacity, tile_rows, columns), lax...]
    unnamed x53 -> x98, local copies, waits for them, and re-layouts: 72.6 us -> 85.5 us
    convert_element_type x1 -> x0, local copies, waits for them, and re-layouts: 10.6 us -> none  [on_device(): outgoing = jnp.einsum('pu,vxuyz->pxvyz', placing, blocks, preferred_eleme...]
    reshape x1, local copies, waits for them, and re-layouts: 11.1 us -> 1.11 us  [on_device(): jnp.concatenate(lax.all_to_all(jnp.stack(jnp.split(outgoing.reshape(slab_...]
  transfers between devices with their start and end apart: 9 -> 9, of which waited for: 4 -> 4; matrix products, arithmetic and copies ran while one was open for 20% -> 18% of each run, Pallas kernels for 0% -> 0%
where the time goes in v1:
time: 572 us; the launch traced here: 563 us
  local copies, waits for them, and re-layouts  200 us (35%)
  waiting for transfers between devices  162 us (28%)
  matrix products  84.2 us (15%)
  blocking collectives  78.8 us (14%)
  starting transfers between devices  17.4 us (3%)
  between operations  15.3 us (3%)
    psum x1, waiting for transfers between devices, on_device(): gram = lax.psum(partial_value, ('grp', 'gx', 'gy'))  145 us
    unnamed x98, local copies, waits for them, and re-layouts  85.5 us
    all_to_all x1, blocking collectives, on_device(): lax.all_to_all(jnp.stack(jnp.split(outgoing.reshape(slab_count, capacity,...  78.8 us
    dot_general x2, matrix products, tendency(): jnp.einsum('kj,jxyz->kxyz', reaction, center, precision=lax.Precision.HIG...  63 us
    slice x16, local copies, waits for them, and re-layouts, tendency(): jnp.roll(center, offset, 3)  52.2 us
    another operation x17, local copies, waits for them, and re-layouts, on_device(): jnp.stack(jnp.split(outgoing.reshape(slab_count, capacity, tile_rows, col...  27.4 us
    split x17, local copies, waits for them, and re-layouts, on_device(): jnp.split(outgoing.reshape(slab_count, capacity, tile_rows, columns), lax...  25.5 us
    ppermute x4, starting transfers between devices, extended(): after = lax.ppermute(initial, axis, down)  13.9 us
  transfers between devices with their start and end apart: 9, of which 4 were waited for; matrix products, arithmetic and copies ran while one was open for 18% of the time, Pallas kernels for 0%

profile of v1, /device:TPU:1, one launch (start us, length us, event | category | flops | bytes accessed | tf_op | source)
XLA Modules:
  0.0 562.6 jit_solution(14622110362047146983)
XLA Ops:
  9.2 3.0 collective-permute-start.1
  13.1 5.8 %fusion.115 = (f32[8,48,16,1]{3,2,1,0:T(8,128)S(1)}, f32[8,48,16,1]{3,2,1,0:T(8,128)}) fusion(f32[8,48,16,128]{3,2,1,0:T(8,128)} %param.6), kind=kLoop, calls=%fused_computation.247 | loop fusion | bytes 98304 | tf_op jit(solution)/shard_map/jit(_roll_static)/slice | solution.py:55
  18.8 3.9 fusion.116
  23.8 3.7 fusion.114
  32.6 5.7 %constant_dynamic-update-slice_fusion.1 = (f32[8,52,16,128]{3,0,2,1:T(8,128)}, f32[8,52,16,128]{3,0,2,1:T(8,128)}, f32[8,56,16,128]{3,0,2,1:T(8,128)}) fusion(f32[8,48,16,128]{3,2,1,0:T(8,128)S(1)} %copy-done.1, f32[8,52,16,128]{3,0,2,1:T(8,128)} %get-tuple-element.71, f32[8,56,16,128]{3,0,2,1:T(8,128)} %get-tuple-element.72), kind=kLoop, calls=%fused_computation.168 | loop fusion | bytes 12582912
  39.2 2.9 fusion.99
  42.1 5.8 %collective-permute-start.2 = (f32[8,56,4,128]{3,0,2,1:T(8,128)}, f32[8,56,4,128]{3,0,2,1:T(8,128)}, u32[]{:S(2)}, u32[]{:S(2)}) collective-permute-start(f32[8,56,4,128]{3,0,2,1:T(8,128)} %get-tuple-element.28), channel_id=1, source_target_pairs={{1,0},{2,1},{3,2},{4,3},{5,4},{6,5},{7,6},{0,7},{9,8},{10,9},{11,1... | collective-permute-start | bytes 2752520 | tf_op jit(solution)/shard_map/ppermute | solution.py:26
  48.0 3.8 fusion.110
  51.8 5.6 copy.135
  57.4 3.5 copy.136
  60.9 3.5 copy.137
  64.4 3.5 copy.138
  68.0 3.6 copy.139
  71.6 3.6 copy.140
  75.2 3.5 copy.141
  78.7 3.5 copy.142
  82.1 3.5 copy.143
  85.6 3.5 copy.144
  89.0 3.5 copy.145
  92.5 3.8 copy.146
  96.3 3.5 copy.147
  99.8 3.4 copy.148
  103.3 3.5 copy.149
  106.8 3.4 copy.150
  111.8 37.5 %fusion.43 = f32[8,48,16,128]{3,0,2,1:T(8,128)S(1)} fusion(f32[8,56,16,128]{3,0,2,1:T(8,128)} %get-tuple-element.70, f32[8,56,4,128]{3,0,2,1:T(8,128)} %collective-permute-done.3, f32[8,56,4,128]{3,0,2,1:T(8,128)} %collective-permute-done.2, f32[8,52,16,128]{3,0,2,1:T(8,128)} %get-tuple-element.65, f32[8,52,16,128]{3,0,2,1:T(8,128)} %get-tuple-element.69, ...), kind=kOutput, calls=%fused_computation.70 | convolution fusion | flops 128974848 | bytes 90440736 | tf_op jit(solution)/shard_map/kj,jxyz->kxyz/dot_general | solution.py:40
  149.4 3.8 fusion.100
  153.2 3.8 fusion.101
  157.0 3.8 fusion.102
  160.9 3.9 fusion.103
  164.8 3.8 fusion.104
  168.6 2.8 collective-permute-start.4
  171.3 3.9 fusion.105
  175.3 2.1 collective-permute-done.5
  177.5 5.4 collective-permute-start.6
  183.2 3.8 fusion.106
  186.9 3.9 fusion.107
  190.9 9.9 %collective-permute-done.6 = f32[8,56,4,128]{3,0,2,1:T(8,128)S(1)} collective-permute-done((f32[8,56,4,128]{3,0,2,1:T(8,128)S(1)}, f32[8,56,4,128]{3,0,2,1:T(8,128)S(1)}, u32[]{:S(2)}, u32[]{:S(2)}) %collective-permute-start.6) | collective-permute-done | bytes 917536 | tf_op jit(solution)/shard_map/ppermute | solution.py:26
  200.7 5.7 %collective-permute-done.7 = f32[8,56,4,128]{3,0,2,1:T(8,128)S(1)} collective-permute-done((f32[8,56,4,128]{3,0,2,1:T(8,128)S(1)}, f32[8,56,4,128]{3,0,2,1:T(8,128)S(1)}, u32[]{:S(2)}, u32[]{:S(2)}) %collective-permute-start.7) | collective-permute-done | bytes 917536 | tf_op jit(solution)/shard_map/ppermute | solution.py:25
  206.4 3.9 pad_maximum_fusion
  210.4 25.4 %fusion.118 = (bf16[8,48,16,128]{3,0,2,1:T(8,128)(2,1)S(1)}, f32[8,48,16,128]{3,0,2,1:T(8,128)}) fusion(f32[8,48,16,128]{3,0,2,1:T(8,128)S(1)} %fusion.43, f32[8,48,16,124]{3,0,2,1:T(8,128)} %get-tuple-element.32, f32[8,48,16,4]{3,0,2,1:T(8,128)} %get-tuple-element.30, f32[8]{0:T(128)S(1)} %get-tuple-element.78, f32[8,48,16,4]{3,0,2,1:T(8,128)} %get-tuple-element.31, ...), kind=kOutput, calls=%fused_computation.250 | convolution fusion | flops 131334144 | bytes 65028608 | tf_op jit(solution)/shard_map/kj,jxyz->kxyz/dot_general | solution.py:40
  237.7 7.7 %fusion.98 = (bf16[2,48,8,2,128]{4,0,3,1,2:T(2,128)(2,1)S(1)}, bf16[2,48,8,2,128]{4,0,3,1,2:T(2,128)(2,1)S(1)}, bf16[2,48,8,2,128]{4,0,3,1,2:T(2,128)(2,1)S(1)},...) fusion(bf16[32,48,8,2,128]{4,0,3,1,2:T(8,128)(2,1)S(1)} %conver, ...), kind=kLoop, calls=%fused_computation.230 | loop fusion | bytes 12582912 | tf_op jit(solution)/shard_map/split | solution.py:93
  246.3 2.0 stack.51
  250.1 1.9 copy.106
  252.1 2.0 stack.52
  256.1 2.1 stack.53
  258.1 1.9 copy.108
  260.1 2.0 stack.54
  262.1 2.0 copy.109
  264.0 2.0 stack.55
  268.0 2.1 stack.56
  270.1 2.0 copy.111
  272.0 2.0 stack.57
  274.1 2.0 copy.112
  276.0 2.0 stack.58
  279.1 2.0 stack.59
  289.6 2.1 stack.66
  303.5 78.8 %all_to_all.5 = bf16[16,1,2,48,2048]{4,3,2,1,0:T(8,128)(2,1)S(1)} all-to-all(bf16[16,1,2,48,2048]{4,3,2,1,0:T(8,128)(2,1)} %constant_dynamic-update-slice_fusion.7), channel_id=1, replica_groups=mesh['grp'=4,'gx'=4,'gy'=8] {'grp','gx'}, dimensions={0} | all-to-all | bytes 12582912 | tf_op jit(solution)/shard_map/all_to_all | solution.py:91
  383.4 2.7 copy-done.3
  386.1 6.5 %convolution_bitcast_fusion.1 = f32[768,768]{1,0:T(8,128)} fusion(bf16[2,768,2048]{2,1,0:T(8,128)(2,1)S(1)} %bitcast.93), kind=kOutput, calls=%fused_computation.147 | convolution fusion | flops 4831838208 | bytes 8650752 | tf_op jit(solution)/shard_map/dot_general | solution.py:106
  392.6 2.2 copy.122
  394.9 144.6 %all-reduce.2.cloned.1.call-done = f32[768,768]{1,0:T(8,128)} async-done(((f32[768,768]{1,0:T(8,128)}), f32[768,768]{1,0:T(8,128)}) %all-reduce.2.cloned.1.call-update) | async-done | bytes 2359312 | tf_op jit(solution)/shard_map/psum | solution.py:109
  539.5 4.6 multiply_reduce_fusion
  549.1 4.0 convolution_bitcast_fusion
  553.1 2.5 reshape.163
  (133 shorter events, 47.1 us)
Async XLA Ops:
  7.2 532.3 %copy-start = (f32[768,96]{0,1:T(8,128)S(1)}, f32[768,96]{0,1:T(8,128)}, u32[]{:S(2)}) copy-start(f32[768,96]{0,1:T(8,128)} %param.10) | copy-start | bytes 884740
  7.2 532.3 %all-reduce.2.cloned.1.call-start = ((), (), s32[]{:S(2)}) async-start(), calls=%async_computation.1 | async-start | bytes 4718592 | tf_op jit(solution)/shard_map/psum | solution.py:109
  9.2 21.6 %collective-permute-start.1 = (f32[8,4,16,128]{3,0,2,1:T(8,128)}, f32[8,4,16,128]{3,0,2,1:T(8,128)}, u32[]{:S(2)}, u32[]{:S(2)}) collective-permute-start(f32[8,4,16,128]{3,0,2,1:T(8,128)} %copy.133), channel_id=1, source_target_pairs={{0,8},{8,16},{16,24},{24,32},{32,40},{40,48},{48,56},{56,64},{64,7... | collective-permute-start | bytes 786440 | tf_op jit(solution)/shard_map/ppermute | solution.py:25
  13.1 5.8 %copy-start.1 = (f32[8,48,16,128]{3,2,1,0:T(8,128)S(1)}, f32[8,48,16,128]{3,2,1,0:T(8,128)}, u32[]{:S(2)}) copy-start(f32[8,48,16,128]{3,2,1,0:T(8,128)} %param.6) | copy-start | bytes 9437188
  13.1 25.3 %collective-permute-start = (f32[8,4,16,128]{3,0,2,1:T(8,128)}, f32[8,4,16,128]{3,0,2,1:T(8,128)S(1)}, u32[]{:S(2)}, u32[]{:S(2)}) collective-permute-start(f32[8,4,16,128]{3,0,2,1:T(8,128)} %copy.134), channel_id=1, source_target_pairs={{8,0},{16,8},{24,16},{32,24},{40,32},{48,40},{56,48},{64,56},{72,6... | collective-permute-start | bytes 786440 | tf_op jit(solution)/shard_map/ppermute | solution.py:26
  42.1 69.7 %collective-permute-start.2 = (f32[8,56,4,128]{3,0,2,1:T(8,128)}, f32[8,56,4,128]{3,0,2,1:T(8,128)}, u32[]{:S(2)}, u32[]{:S(2)}) collective-permute-start(f32[8,56,4,128]{3,0,2,1:T(8,128)} %get-tuple-element.28), channel_id=1, source_target_pairs={{1,0},{2,1},{3,2},{4,3},{5,4},{6,5},{7,6},{0,7},{9,8},{10,9},{11,1... | collective-permute-start | bytes 2752520 | tf_op jit(solution)/shard_map/ppermute | solution.py:26
  47.9 64.0 %collective-permute-start.3 = (f32[8,56,4,128]{3,0,2,1:T(8,128)}, f32[8,56,4,128]{3,0,2,1:T(8,128)}, u32[]{:S(2)}, u32[]{:S(2)}) collective-permute-start(f32[8,56,4,128]{3,0,2,1:T(8,128)} %get-tuple-element.29), channel_id=1, source_target_pairs={{0,1},{1,2},{2,3},{3,4},{4,5},{5,6},{6,7},{7,0},{8,9},{9,10},{10,1... | collective-permute-start | bytes 2752520 | tf_op jit(solution)/shard_map/ppermute | solution.py:25
  51.8 5.6 copy-start.7
  57.4 3.5 copy-start.6
  68.0 3.6 copy-start.5
  71.6 3.6 copy-start.4
  96.3 3.5 copy-start.9
  99.8 3.4 copy-start.8
  106.8 5.0 copy-start.28
  106.8 5.0 copy-start.29
  106.8 5.0 copy-start.30
  168.6 6.7 %collective-permute-start.4 = (f32[8,4,16,128]{3,0,2,1:T(8,128)S(1)}, f32[8,4,16,128]{3,0,2,1:T(8,128)S(1)}, u32[]{:S(2)}, u32[]{:S(2)}) collective-permute-start(f32[8,4,16,128]{3,0,2,1:T(8,128)S(1)} %get-tuple-element.46), channel_id=1, source_target_pairs={{8,0},{16,8},{24,16},{32,24},{40,32},{48,40},{56,48},{64,56},{72,6... | collective-permute-start | bytes 786440 | tf_op jit(solution)/shard_map/ppermute | solution.py:26
  171.3 6.0 %collective-permute-start.5 = (f32[8,4,16,128]{3,0,2,1:T(8,128)S(1)}, f32[8,4,16,128]{3,0,2,1:T(8,128)S(1)}, u32[]{:S(2)}, u32[]{:S(2)}) collective-permute-start(f32[8,4,16,128]{3,0,2,1:T(8,128)S(1)} %get-tuple-element.47), channel_id=1, source_target_pairs={{0,8},{8,16},{16,24},{24,32},{32,40},{40,48},{48,56},{56,64},{64,7... | collective-permute-start | bytes 786440 | tf_op jit(solution)/shard_map/ppermute | solution.py:25
  175.3 31.2 %copy-start.26 = (f32[8,4,16,128]{3,0,2,1:T(8,128)}, f32[8,4,16,128]{3,0,2,1:T(8,128)S(1)}, u32[]{:S(2)}) copy-start(f32[8,4,16,128]{3,0,2,1:T(8,128)S(1)} %collective-permute-done.4) | copy-start | bytes 786436
  177.4 29.1 %copy-start.27 = (f32[8,4,16,128]{3,0,2,1:T(8,128)}, f32[8,4,16,128]{3,0,2,1:T(8,128)S(1)}, u32[]{:S(2)}) copy-start(f32[8,4,16,128]{3,0,2,1:T(8,128)S(1)} %collective-permute-done.5) | copy-start | bytes 786436
  177.5 23.2 %collective-permute-start.6 = (f32[8,56,4,128]{3,0,2,1:T(8,128)S(1)}, f32[8,56,4,128]{3,0,2,1:T(8,128)S(1)}, u32[]{:S(2)}, u32[]{:S(2)}) collective-permute-start(f32[8,56,4,128]{3,0,2,1:T(8,128)S(1)} %get-tuple-element.26), channel_id=1, source_target_pairs={{1,0},{2,1},{3,2},{4,3},{5,4},{6,5},{7,6},{0,7},{9,8},{10,9},{11,1... | collective-permute-start | bytes 2752520 | tf_op jit(solution)/shard_map/ppermute | solution.py:26
  182.9 23.5 %collective-permute-start.7 = (f32[8,56,4,128]{3,0,2,1:T(8,128)S(1)}, f32[8,56,4,128]{3,0,2,1:T(8,128)S(1)}, u32[]{:S(2)}, u32[]{:S(2)}) collective-permute-start(f32[8,56,4,128]{3,0,2,1:T(8,128)S(1)} %get-tuple-element.27), channel_id=1, source_target_pairs={{0,1},{1,2},{2,3},{3,4},{4,5},{5,6},{6,7},{7,0},{8,9},{9,10},{10,1... | collective-permute-start | bytes 2752520 | tf_op jit(solution)/shard_map/ppermute | solution.py:25
  190.8 19.5 %copy-start.2 = (f32[8,48,16,128]{3,2,1,0:T(8,128)S(1)}, f32[8,48,16,128]{3,2,1,0:T(8,128)}, u32[]{:S(2)}) copy-start(f32[8,48,16,128]{3,2,1,0:T(8,128)} %param.6) | copy-start | bytes 9437188
  284.8 6.9 %copy-start.11 = (bf16[1,1,2,48,2048]{4,3,2,1,0:T(8,128)(2,1)S(1)}, bf16[1,1,2,48,2048]{4,3,2,1,0:T(8,128)(2,1)}, u32[]{:S(2)}) copy-start(bf16[1,1,2,48,2048]{4,3,2,1,0:T(8,128)(2,1)} %stack.52) | copy-start | bytes 1179652
  285.0 7.4 %copy-start.12 = (bf16[1,1,2,48,2048]{4,3,2,1,0:T(8,128)(2,1)S(1)}, bf16[1,1,2,48,2048]{4,3,2,1,0:T(8,128)(2,1)}, u32[]{:S(2)}) copy-start(bf16[1,1,2,48,2048]{4,3,2,1,0:T(8,128)(2,1)} %stack.53) | copy-start | bytes 1179652
  286.1 7.2 %copy-start.13 = (bf16[1,1,2,48,2048]{4,3,2,1,0:T(8,128)(2,1)S(1)}, bf16[1,1,2,48,2048]{4,3,2,1,0:T(8,128)(2,1)}, u32[]{:S(2)}) copy-start(bf16[1,1,2,48,2048]{4,3,2,1,0:T(8,128)(2,1)} %stack.54) | copy-start | bytes 1179652
  286.3 7.8 %copy-start.14 = (bf16[1,1,2,48,2048]{4,3,2,1,0:T(8,128)(2,1)S(1)}, bf16[1,1,2,48,2048]{4,3,2,1,0:T(8,128)(2,1)}, u32[]{:S(2)}) copy-start(bf16[1,1,2,48,2048]{4,3,2,1,0:T(8,128)(2,1)} %stack.55) | copy-start | bytes 1179652
  287.3 7.5 %copy-start.15 = (bf16[1,1,2,48,2048]{4,3,2,1,0:T(8,128)(2,1)S(1)}, bf16[1,1,2,48,2048]{4,3,2,1,0:T(8,128)(2,1)}, u32[]{:S(2)}) copy-start(bf16[1,1,2,48,2048]{4,3,2,1,0:T(8,128)(2,1)} %stack.56) | copy-start | bytes 1179652
  287.5 8.1 %copy-start.16 = (bf16[1,1,2,48,2048]{4,3,2,1,0:T(8,128)(2,1)S(1)}, bf16[1,1,2,48,2048]{4,3,2,1,0:T(8,128)(2,1)}, u32[]{:S(2)}) copy-start(bf16[1,1,2,48,2048]{4,3,2,1,0:T(8,128)(2,1)} %stack.57) | copy-start | bytes 1179652
  288.6 7.8 %copy-start.17 = (bf16[1,1,2,48,2048]{4,3,2,1,0:T(8,128)(2,1)S(1)}, bf16[1,1,2,48,2048]{4,3,2,1,0:T(8,128)(2,1)}, u32[]{:S(2)}) copy-start(bf16[1,1,2,48,2048]{4,3,2,1,0:T(8,128)(2,1)} %stack.58) | copy-start | bytes 1179652
  289.6 7.6 %copy-start.18 = (bf16[1,1,2,48,2048]{4,3,2,1,0:T(8,128)(2,1)S(1)}, bf16[1,1,2,48,2048]{4,3,2,1,0:T(8,128)(2,1)}, u32[]{:S(2)}) copy-start(bf16[1,1,2,48,2048]{4,3,2,1,0:T(8,128)(2,1)} %stack.59) | copy-start | bytes 1179652
  291.7 6.3 %copy-start.19 = (bf16[1,1,2,48,2048]{4,3,2,1,0:T(8,128)(2,1)S(1)}, bf16[1,1,2,48,2048]{4,3,2,1,0:T(8,128)(2,1)}, u32[]{:S(2)}) copy-start(bf16[1,1,2,48,2048]{4,3,2,1,0:T(8,128)(2,1)} %stack.60) | copy-start | bytes 1179652
  292.5 6.3 %copy-start.20 = (bf16[1,1,2,48,2048]{4,3,2,1,0:T(8,128)(2,1)S(1)}, bf16[1,1,2,48,2048]{4,3,2,1,0:T(8,128)(2,1)}, u32[]{:S(2)}) copy-start(bf16[1,1,2,48,2048]{4,3,2,1,0:T(8,128)(2,1)} %stack.61) | copy-start | bytes 1179652
  293.3 6.3 %copy-start.21 = (bf16[1,1,2,48,2048]{4,3,2,1,0:T(8,128)(2,1)S(1)}, bf16[1,1,2,48,2048]{4,3,2,1,0:T(8,128)(2,1)}, u32[]{:S(2)}) copy-start(bf16[1,1,2,48,2048]{4,3,2,1,0:T(8,128)(2,1)} %stack.62) | copy-start | bytes 1179652
  294.1 6.3 %copy-start.22 = (bf16[1,1,2,48,2048]{4,3,2,1,0:T(8,128)(2,1)S(1)}, bf16[1,1,2,48,2048]{4,3,2,1,0:T(8,128)(2,1)}, u32[]{:S(2)}) copy-start(bf16[1,1,2,48,2048]{4,3,2,1,0:T(8,128)(2,1)} %stack.63) | copy-start | bytes 1179652
  294.8 6.3 %copy-start.23 = (bf16[1,1,2,48,2048]{4,3,2,1,0:T(8,128)(2,1)S(1)}, bf16[1,1,2,48,2048]{4,3,2,1,0:T(8,128)(2,1)}, u32[]{:S(2)}) copy-start(bf16[1,1,2,48,2048]{4,3,2,1,0:T(8,128)(2,1)} %stack.64) | copy-start | bytes 1179652
  295.6 6.3 %copy-start.24 = (bf16[1,1,2,48,2048]{4,3,2,1,0:T(8,128)(2,1)S(1)}, bf16[1,1,2,48,2048]{4,3,2,1,0:T(8,128)(2,1)}, u32[]{:S(2)}) copy-start(bf16[1,1,2,48,2048]{4,3,2,1,0:T(8,128)(2,1)} %stack.65) | copy-start | bytes 1179652
  296.4 6.3 %copy-start.25 = (bf16[1,1,2,48,2048]{4,3,2,1,0:T(8,128)(2,1)S(1)}, bf16[1,1,2,48,2048]{4,3,2,1,0:T(8,128)(2,1)}, u32[]{:S(2)}) copy-start(bf16[1,1,2,48,2048]{4,3,2,1,0:T(8,128)(2,1)} %stack.66) | copy-start | bytes 1179652
  383.4 2.7 copy-start.3
  386.1 6.5 %copy-start.10 = (f32[8,48,16,128]{3,0,2,1:T(8,128)S(1)}, f32[8,48,16,128]{3,0,2,1:T(8,128)}, u32[]{:S(2)}) copy-start(f32[8,48,16,128]{3,0,2,1:T(8,128)} %get-tuple-element.99) | copy-start | bytes 9437188
Sparse Core Ops, SparseCore 0:
  392.7 146.7 all-reduce.1
